TPU v7x, 1024 devices: a whole 4x4x32 slice. The times are simulated.
1024 devices in a mesh: dp: 8 (over y_lo, x), mp: 128 (over y_hi, z, core).
Axes of the slice: x: 4, y: 4 (y_hi: 2, y_lo: 2; y = y_hi * 2 + y_lo), z: 32, core: 2. Of those that a mesh axis runs over, the one named last changes fastest.
Arguments:
- tokens_in: bfloat16 [1024, 6144], P('dp', 'mp'), may hold values from -6 to 6
- in_weight: bfloat16 [6144, 24576], P(None, 'mp'), may hold values from -0.3125 to 0.3125
- hidden_grad: bfloat16 [1024, 24576], P('dp', 'mp'), may hold values from -4 to 4
Outputs:
- token_grad: bfloat16 [1024, 6144], P('dp', 'mp')
- weight_grad: float32 [6144, 24576], P('dp', 'mp')
All inputs are finite; a program needn't handle non-finite values.
Results may differ from a plain program's by a relative error of at most 0.015.
Values may be sent and summed in bfloat16 or wider, within the bound.
A program may use at most 32 MiB of HBM per device.

v0:
```python
import jax
import jax.numpy as jnp
from jax import lax
from jax.sharding import PartitionSpec as P


def gelu_slope(value):
    normal_cdf = 0.5 * (1.0 + lax.erf(value * 0.7071067811865476))
    density = jnp.exp(-0.5 * value * value) * 0.3989422804014327
    return normal_cdf + value * density


def local(tokens_in, in_weight, hidden_grad):
    gathered = lax.all_gather(tokens_in, "mp", axis=1, tiled=True)
    preact = jnp.dot(gathered, in_weight, preferred_element_type=jnp.float32)
    pre_grad = (hidden_grad.astype(jnp.float32) * gelu_slope(preact)).astype(jnp.bfloat16)
    token_rows = lax.psum_scatter(
        lax.dot_general(
            in_weight, pre_grad, (((1,), (1,)), ((), ())), preferred_element_type=jnp.float32
        ),
        "mp",
        scatter_dimension=0,
        tiled=True,
    )
    token_grad = token_rows.T.astype(jnp.bfloat16)
    weight_grad = lax.psum_scatter(
        lax.dot_general(
            gathered, pre_grad, (((0,), (0,)), ((), ())), preferred_element_type=jnp.float32
        ).astype(jnp.bfloat16),
        "dp",
        scatter_dimension=0,
        tiled=True,
    ).astype(jnp.float32)
    return (token_grad, weight_grad)


def solution(mesh):
    in_specs = (P("dp", "mp"), P(None, "mp"), P("dp", "mp"))
    out_specs = (P("dp", "mp"), P("dp", "mp"))
    return jax.shard_map(local, mesh=mesh, in_specs=in_specs, out_specs=out_specs, check_vma=False)
```

profile of v0, /device:TPU:1, one launch (start us, length us, event | category | flops | bytes accessed | tf_op | source)
XLA Modules:
  0.0 758.4 jit_solution(7936130286065482145)
XLA Ops:
  7.2 0.0 copy-start
  7.2 0.0 all-gather.2.cloned.1.call-start
  7.2 0.7 all-gather.2.cloned.1.call-update
  7.9 0.0 copy-start.1
  7.9 0.0 reduce-scatter.7.cloned.1.call-start
  8.0 279.3 %all-gather.2.cloned.1.call-done = bf16[128,6144]{0,1:T(8,128)(2,1)} async-done(((bf16[128,48]{0,1:T(8,128)(2,1)}), bf16[128,6144]{0,1:T(8,128)(2,1)}) %all-gather.2.cloned.1.call-update) | async-done | bytes 1572880 | tf_op jit(solution)/shard_map/all_gather | solution.py:14
  287.2 0.0 copy-done
  287.2 2.2 fusion.31
  289.4 0.0 copy-done.1
  289.4 2.3 convolution_bitcast_fusion
  291.7 3.5 copy.7
  295.3 0.0 reduce-scatter.7.cloned.1.call-update
  295.3 0.0 reduce-scatter.5.cloned.1.call-start
  295.4 3.6 fusion
  299.0 0.0 reduce-scatter.5.cloned.1.call-update
  299.0 372.1 %reduce-scatter.7.cloned.1.call-done = f32[48,128]{1,0:T(8,128)} async-done(((f32[6144,128]{1,0:T(8,128)}), f32[48,128]{1,0:T(8,128)}) %reduce-scatter.7.cloned.1.call-update) | async-done | bytes 24592
  671.1 0.8 copy.8
  671.9 0.7 copy.6
  672.6 77.4 %reduce-scatter.5.cloned.1.call-done = bf16[768,192]{0,1:T(8,128)(2,1)} async-done(((bf16[6144,192]{0,1:T(8,128)(2,1)}), bf16[768,192]{0,1:T(8,128)(2,1)}) %reduce-scatter.5.cloned.1.call-update) | async-done | bytes 294928 | tf_op jit(solution)/shard_map/reduce_scatter | solution.py:26
  750.1 1.8 convert_element_type.27
Async XLA Ops:
  7.2 280.1 %copy-start = (bf16[6144,192]{0,1:T(8,128)(2,1)S(1)}, bf16[6144,192]{0,1:T(8,128)(2,1)}, u32[]{:S(2)}) copy-start(bf16[6144,192]{0,1:T(8,128)(2,1)} %param.4) | copy-start | bytes 7077892
  7.2 280.0 %all-gather.2.cloned.1.call-start = ((), (), s32[]{:S(2)}) async-start(), calls=%async_computation.2 | async-start | bytes 1585152 | tf_op jit(solution)/shard_map/all_gather | solution.py:14
  7.9 281.5 %copy-start.1 = (bf16[128,192]{0,1:T(8,128)(2,1)S(1)}, bf16[128,192]{0,1:T(8,128)(2,1)}, u32[]{:S(2)}) copy-start(bf16[128,192]{0,1:T(8,128)(2,1)} %param.5) | copy-start | bytes 147460
  7.9 663.2 %reduce-scatter.7.cloned.1.call-start = ((), (), s32[]{:S(2)}) async-start(), calls=%async_computation.4 | async-start | bytes 3170304
  295.3 454.8 %reduce-scatter.5.cloned.1.call-start = ((), (), s32[]{:S(2)}) async-start(), calls=%async_computation.3 | async-start | bytes 2654208 | tf_op jit(solution)/shard_map/reduce_scatter | solution.py:26
Sparse Core Ops, SparseCore 0:
  12.4 274.8 all-gather.1
  295.4 375.6 reduce-scatter.6
  674.5 75.4 reduce-scatter.4
where the time goes:
time: 762 us; the launch traced here: 758 us
  waiting for transfers between devices  729 us (96%)
  between operations  13.8 us (2%)
  matrix products  8.14 us (1%)
    unnamed x4, waiting for transfers between devices  373 us
    all_gather x1, waiting for transfers between devices, local(): gathered = lax.all_gather(tokens_in, 'mp', axis=1, tiled=True)  279 us
    reduce_scatter x1, waiting for transfers between devices, local(): lax.psum_scatter(lax.dot_general(gathered, pre_grad, (((0,), (0,)), ((),...  77.4 us
  transfers between devices with their start and end apart: 3, of which 3 were waited for; matrix products, arithmetic and copies ran while one was open for 1% of the time, Pallas kernels for 0%

commit v1 on v0

v1 whole, which is shorter than its diff:
```python
import jax
import jax.numpy as jnp
from jax import lax
from jax.experimental import pallas as pl
from jax.experimental.pallas import tpu as pltpu
from jax.sharding import PartitionSpec as P

MESH = pl.DeviceIdType.MESH
F32, BF16 = jnp.float32, jnp.bfloat16

NY, NG, NN, NC, NZ, NDP = 2, 8, 4, 2, 32, 8
CH, TOK, HID = 48, 128, 192
BLK = NN * NC * CH
NEAR = range(1, 8)


def gelu_slope(value):
    normal_cdf = 0.5 * (1.0 + lax.erf(value * 0.7071067811865476))
    density = jnp.exp(-0.5 * value * value) * 0.3989422804014327
    return normal_cdf + value * density


def ring(i):
    return ((i + 1) // 2) * (2 * (i % 2) - 1)


def kernel(
    x_ref, w_hbm, h_ref, tok_ref, wg_hbm,
    w, xt, acc, hgt, tp, sr, pair, near_in, far_out, far_in, xs, pga, wg,
    w_sem, wg_sem, own_sem,
    agf_s, agf_r, agn_s, agn_r, agc_s, agc_r,
    rsc_s, rsc_r, rsn_s, rsn_r, rsf_s, rsf_r,
    pg_s, pg_r, xs_s, xs_r, xc_s, xc_r,
):
    dp, mp = lax.axis_index("dp"), lax.axis_index("mp")
    yh, z, c = mp // 64, (mp // 2) % NZ, mp % 2
    g0, n = z // NN, z % NN
    sgn = 1 - 2 * c

    def at(dz, dy=0, core=c):
        return (dp, ((yh + dy) % NY) * 64 + ((z + dz + NZ) % NZ) * 2 + core)

    def send(src, dst, s, r, device):
        return pltpu.make_async_remote_copy(
            src_ref=src, dst_ref=dst, send_sem=s, recv_sem=r, device_id=device, device_id_type=MESH
        )

    def near_off(e):
        return e % 2, (0, 1, -1, 2 * sgn)[e // 2]

    def group(offset):
        return (g0 + offset + NG) % NG

    sibling = at(0, core=1 - c)
    far_z = (8, -8, 4, -4)

    load_w = pltpu.make_async_copy(w_hbm, w, w_sem)
    load_w.start()

    barrier = pltpu.get_barrier_semaphore()
    for dz in far_z:
        pl.semaphore_signal(barrier, inc=1, device_id=at(-dz), device_id_type=MESH)
    for e in NEAR:
        dy, dz = near_off(e)
        pl.semaphore_signal(barrier, inc=1, device_id=at(-dz, dy), device_id_type=MESH)
    pl.semaphore_signal(barrier, inc=1, device_id=sibling, device_id_type=MESH)
    for r in range(1, NDP):
        pl.semaphore_signal(barrier, inc=1, device_id=((dp - r + NDP) % NDP, mp), device_id_type=MESH)

    xt[yh, g0, n, c] = x_ref[...].astype(F32).T.astype(BF16)
    hgt[...] = h_ref[...].astype(F32).T
    acc[...] = jnp.zeros_like(acc)
    pl.semaphore_wait(barrier, 4 + 7 + 1 + 7)

    def ag_far(k):
        chunk = (0, 0, 0, 0, -2, 2, -2 * sgn)[k]
        dz = (8, -8, 4, -4, 4, -4, 8 * sgn)[k]
        ref = xt.at[yh, group(chunk), n, c]
        return send(ref, ref, agf_s.at[k], agf_r.at[k], at(dz))

    def ag_far_got(k):
        chunk = (-2, 2, -1, 1, -3, 3, 4)[k]
        ref = xt.at[yh, group(chunk), n, c]
        send(ref, ref, agf_s.at[k], agf_r.at[k], at(8)).wait_recv()

    def ag_near(g, e):
        dy, dz = near_off(e)
        ref = xt.at[yh, g, n, c]
        return send(ref, ref, agn_s.at[g, e - 1], agn_r.at[g, e - 1], at(dz, dy))

    def ag_near_start(i):
        g = group(ring(i))
        for e in NEAR:
            ag_near(g, e).start()

    def ag_near_got(g):
        for e in NEAR:
            dy, dz = near_off(e)
            ref = xt.at[(yh + dy) % NY, g, (z - dz + NZ) % NN, c]
            send(ref, ref, agn_s.at[g, e - 1], agn_r.at[g, e - 1], at(8)).wait_recv()

    def ag_core(g, core):
        ref = xt.at[:, g, :, core]
        return send(ref, ref, agc_s.at[g], agc_r.at[g], sibling)

    def rows_of(y, g):
        return pl.ds(pl.multiple_of((y * NG + g) * BLK, BLK), BLK)

    def pass_on(i):
        g = group(ring(i))
        ag_near_got(g)
        ag_core(g, c).start()

    def multiply(i):
        g = group(ring(i))
        ag_core(g, 1 - c).wait_recv()
        total = acc[...]
        for y in range(NY):
            total += lax.dot_general(
                w[rows_of(y, g), :], xt[y, g].reshape(BLK, TOK),
                (((0,), (0,)), ((), ())), preferred_element_type=F32,
            )
        acc[...] = total

    def loop(low, high, *steps):
        def body(i, carry):
            for step in steps:
                step(i)
            return carry

        lax.fori_loop(low, high, body, 0)

    for k in range(4):
        ag_far(k).start()
    ag_near_start(0)
    ag_far_got(0)
    ag_far_got(1)
    for k in (6, 4, 5):
        ag_far(k).start()
    ag_far_got(2)
    ag_far_got(3)
    loop(1, 5, ag_near_start)
    load_w.wait()
    pass_on(0)
    ag_far_got(4)
    ag_far_got(5)
    loop(5, 7, ag_near_start)
    ag_far_got(6)
    ag_near_start(7)
    pass_on(1)
    loop(2, 8, pass_on, lambda i: multiply(i - 2))
    multiply(6)
    multiply(7)

    pga[dp] = (hgt[...] * gelu_slope(acc[...])).astype(BF16)
    pgt = pga[dp]

    def rs_core(g):
        return send(tp.at[:, g, :, 1 - c], sr.at[:, g], rsc_s.at[g], rsc_r.at[g], sibling)

    def partial(i):
        g = group(ring(i))
        for y in range(NY):
            part = jnp.dot(w[rows_of(y, g), :], pgt, preferred_element_type=F32)
            tp[y, g] = part.astype(BF16).reshape(NN, NC, CH, TOK)
        rs_core(g).start()

    def rs_near(g, e):
        dy, dz = near_off(e)
        src = pair.at[(yh + dy) % NY, g, (z + dz + NZ) % NN]
        return send(src, near_in.at[g, e - 1], rsn_s.at[g, e - 1], rsn_r.at[g, e - 1], at(dz, dy))

    def pair_up(i):
        g = group(ring(i))
        rs_core(g).wait_recv()
        for y in range(NY):
            pair[y, g] = (tp[y, g, :, c].astype(F32) + sr[y, g].astype(F32)).astype(BF16)
        for e in NEAR:
            rs_near(g, e).start()

    def near_sum(offset):
        g = group(offset)
        total = pair[yh, g, n].astype(F32)
        for e in NEAR:
            rs_near(g, e).wait_recv()
        for e in NEAR:
            total += near_in[g, e - 1].astype(F32)
        return total

    def rs_far(k):
        dz = (8, -8, 8 * sgn, 4, -4, 8 * sgn, -8 * sgn)[k]
        return send(far_out.at[k], far_in.at[k], rsf_s.at[k], rsf_r.at[k], at(dz))

    def rs_far_start(k, value):
        far_out[k] = value.astype(BF16)
        rs_far(k).start()

    def rs_far_got(k):
        rs_far(k).wait_recv()
        return far_in[k].astype(F32)

    def slice_of(p, half):
        return p // 4, 2 * (p % 4) + half

    def pg_send(r):
        return send(pga.at[dp], pga.at[dp], pg_s.at[r - 1], pg_r.at[r - 1], ((dp + r) % NDP, mp))

    def pg_got(r):
        ref = pga.at[(dp - r + NDP) % NDP]
        send(ref, ref, pg_s.at[r - 1], pg_r.at[r - 1], sibling).wait_recv()

    def xs_send(r):
        to = (dp + r) % NDP
        y, g = slice_of(to, c)
        return send(xt.at[y, g], xs.at[dp, c], xs_s.at[r - 1], xs_r.at[r - 1], (to, mp))

    def xs_got(r):
        ref = xs.at[(dp - r + NDP) % NDP, c]
        send(ref, ref, xs_s.at[r - 1], xs_r.at[r - 1], sibling).wait_recv()

    def xc_copy(r, half):
        ref = xs.at[(dp - r + NDP) % NDP, half]
        return send(ref, ref, xc_s.at[r - 1], xc_r.at[r - 1], sibling)

    loop(5, 8, partial)
    loop(3, 5, partial)
    loop(5, 8, pair_up)
    loop(1, 3, partial)
    loop(3, 5, pair_up)
    partial(0)
    loop(1, 3, pair_up)
    pair_up(0)
    own_copies = []
    for half in range(2):
        y, g = slice_of(dp, half)
        own_copies.append(pltpu.make_async_copy(xt.at[y, g], xs.at[dp, half], own_sem.at[half]))
        own_copies[-1].start()
    for r in range(1, NDP):
        pg_send(r).start()
    for r in range(1, NDP):
        xs_send(r).start()

    for k in range(7):
        ag_far(k).wait_send()

    def ag_sent(g):
        for e in NEAR:
            ag_near(g, e).wait_send()
        ag_core(g, c).wait_send()

    loop(0, NG, ag_sent)

    rs_far_start(0, near_sum(3))
    rs_far_start(1, near_sum(-3))
    rs_far_start(2, near_sum(4))
    rs_far_start(6, near_sum(-2 * sgn))
    ahead = near_sum(2 * sgn)
    right, left = near_sum(1), near_sum(-1)
    mine = near_sum(0)
    for r in range(1, NDP):
        xs_got(r)
        xc_copy(r, c).start()
    rs_far_start(3, right + rs_far_got(0))
    rs_far_start(4, left + rs_far_got(1))
    rs_far_start(5, ahead + rs_far_got(2))

    for copy in own_copies:
        copy.wait()
    for r in range(1, NDP):
        pg_got(r)
        xc_copy(r, 1 - c).wait_recv()

    def weight_rows(i):
        half, quarter = i // 2, i % 2
        total = jnp.zeros((BLK // 2, HID), F32)
        for p in range(NDP):
            total += lax.dot_general(
                xs[p, half, pl.ds(2 * quarter, 2)].reshape(BLK // 2, TOK), pga[p],
                (((1,), (1,)), ((), ())), preferred_element_type=F32,
            )
        wg[pl.ds(pl.multiple_of(i * (BLK // 2), BLK // 2), BLK // 2), :] = total

    loop(0, 4, weight_rows)
    store_wg = pltpu.make_async_copy(wg, wg_hbm, wg_sem)
    store_wg.start()

    def rs_sent(g):
        for e in NEAR:
            rs_near(g, e).wait_send()
        rs_core(g).wait_send()

    loop(0, NG, rs_sent)
    for r in range(1, NDP):
        pg_send(r).wait_send()
        xs_send(r).wait_send()
        xc_copy(r, c).wait_send()

    for k in (3, 4, 5, 6):
        mine += rs_far_got(k)
    tok_ref[...] = mine.T.astype(BF16)
    for k in range(7):
        rs_far(k).wait_send()
    store_wg.wait()


def local(tokens_in, in_weight, hidden_grad):
    vmem, dma = pltpu.VMEM, pltpu.SemaphoreType.DMA
    features = in_weight.shape[0]
    return pl.pallas_call(
        kernel,
        out_shape=(
            jax.ShapeDtypeStruct((TOK, CH), BF16),
            jax.ShapeDtypeStruct((features // NDP, HID), F32),
        ),
        in_specs=[
            pl.BlockSpec(memory_space=pltpu.VMEM),
            pl.BlockSpec(memory_space=pl.ANY),
            pl.BlockSpec(memory_space=pltpu.VMEM),
        ],
        out_specs=(pl.BlockSpec(memory_space=pltpu.VMEM), pl.BlockSpec(memory_space=pl.ANY)),
        scratch_shapes=[
            vmem((features, HID), BF16),
            vmem((NY, NG, NN, NC, CH, TOK), BF16),
            vmem((HID, TOK), F32),
            vmem((HID, TOK), F32),
            vmem((NY, NG, NN, NC, CH, TOK), BF16),
            vmem((NY, NG, NN, CH, TOK), BF16),
            vmem((NY, NG, NN, CH, TOK), BF16),
            vmem((NG, 7, CH, TOK), BF16),
            vmem((7, CH, TOK), BF16),
            vmem((7, CH, TOK), BF16),
            vmem((NDP, 2, NN, NC, CH, TOK), BF16),
            vmem((NDP, HID, TOK), BF16),
            vmem((features // NDP, HID), F32),
            dma, dma, dma((2,)),
            dma((7,)), dma((7,)), dma((NG, 7)), dma((NG, 7)), dma((NG,)), dma((NG,)),
            dma((NG,)), dma((NG,)), dma((NG, 7)), dma((NG, 7)), dma((7,)), dma((7,)),
            dma((7,)), dma((7,)), dma((7,)), dma((7,)), dma((7,)), dma((7,)),
        ],
        compiler_params=pltpu.CompilerParams(
            collective_id=0, has_side_effects=True, vmem_limit_bytes=40 * 2**20
        ),
        cost_estimate=pl.CostEstimate(
            flops=6 * TOK * features * HID, bytes_accessed=4 * 2**20, transcendentals=2 * TOK * HID
        ),
    )(tokens_in, in_weight, hidden_grad)


def solution(mesh):
    in_specs = (P("dp", "mp"), P(None, "mp"), P("dp", "mp"))
    out_specs = (P("dp", "mp"), P("dp", "mp"))
    return jax.shard_map(local, mesh=mesh, in_specs=in_specs, out_specs=out_specs, check_vma=False)
```

time: 762 us -> 93.8 us (0.12)
  waiting for transfers between devices: 729 us -> 0 us
  Pallas kernels: 0 us -> 82.9 us
  between operations: 13.8 us -> 0.66 us
  matrix products: 8.14 us -> 0 us
    unnamed x4 -> x0, waiting for transfers between devices: 373 us -> none
    all_gather x1 -> x0, waiting for transfers between devices: 279 us -> none  [local(): gathered = lax.all_gather(tokens_in, 'mp', axis=1, tiled=True)]
    pallas_call x0 -> x1, Pallas kernels: none -> 82.9 us  [local(): pl.pallas_call(kernel, out_shape=(jax.ShapeDtypeStruct((TOK, CH), BF16),...]
    reduce_scatter x1 -> x0, waiting for transfers between devices: 77.4 us -> none  [local(): lax.psum_scatter(lax.dot_general(gathered, pre_grad, (((0,), (0,)), ((),...]
    dot_general x3 -> x0, matrix products: 8.14 us -> none  [the longest x1 3.64 us: local(): lax.dot_general(gathered, pre_grad, (((0,), (0,)), ((), ())), preferred_e...]
  transfers between devices with their start and end apart: 3 -> 0, of which waited for: 3 -> 0; matrix products, arithmetic and copies ran while one was open for 1% -> 0% of each run, Pallas kernels for 0% -> 0%
where the time goes in v1:
time: 93.8 us; the launch traced here: 92 us
  Pallas kernels  82.9 us (88%)
  local copies, waits for them, and re-layouts  8.5 us (9%)
    pallas_call x1, Pallas kernels, local(): pl.pallas_call(kernel, out_shape=(jax.ShapeDtypeStruct((TOK, CH), BF16),...  82.9 us
    unnamed x5, local copies, waits for them, and re-layouts  5.61 us
    pallas_call x2, local copies, waits for them, and re-layouts, local(): pl.pallas_call(kernel, out_shape=(jax.ShapeDtypeStruct((TOK, CH), BF16),...  2.88 us

profile of v1, /device:TPU:1, one launch (start us, length us, event | category | flops | bytes accessed | tf_op | source)
XLA Modules:
  0.0 92.0 jit_solution(9785922516418897535)
XLA Ops:
  0.6 0.8 copy.5.x_ref
  1.4 0.9 copy.7.h_ref
  2.4 3.0 %copy.6.w_hbm = bf16[6144,192]{1,0:T(8,128)(2,1)S(1)} copy(bf16[6144,192]{0,1:T(8,128)(2,1)} %param.4) | data formatting | bytes 4718592 | tf_op args[1]
  5.4 82.9 %shard_map.50 = (bf16[128,48]{1,0:T(8,128)(2,1)S(1)}, f32[768,192]{1,0:T(8,128)S(1)}) custom-call(bf16[128,48]{1,0:T(8,128)(2,1)S(1)} %copy.5.x_ref, bf16[6144,192]{1,0:T(8,128)(2,1)S(1)} %copy.6.w_hbm, bf16[128,192]{1,0:T(8,128)(2,1)S(1)} %copy.7.h_ref), custom_call_target="tpu_custom_call" | custom-call | flops 905969664 | bytes 4194304 | tf_op jit(solution)/shard_map/pallas_call | solution.py:309
  88.2 0.0 copy-start
  88.3 0.9 copy-done
  89.1 0.7 copy.8
  89.8 2.2 %copy.9 = f32[768,192]{0,1:T(8,128)} copy(f32[768,192]{1,0:T(8,128)} %copy-done) | data formatting | bytes 1179648 | tf_op jit(solution)/shard_map/pallas_call | solution.py:309
Async XLA Ops:
  88.2 0.9 copy-start

commit v2 on v1

--- a/solution.py
+++ b/solution.py
@@ -25,9 +25,9 @@
 
 
 def kernel(
-    x_ref, w_hbm, h_ref, tok_ref, wg_hbm,
-    w, xt, acc, hgt, tp, sr, pair, near_in, far_out, far_in, xs, pga, wg,
-    w_sem, wg_sem, own_sem,
+    x_hbm, w_hbm, h_hbm, tok_hbm, wg_hbm,
+    w, wt, hg, tok, xt, acc, tp, sr, pair, near_in, far_out, far_in, xs, pga, wg,
+    in_sem, out_sem, own_sem,
     agf_s, agf_r, agn_s, agn_r, agc_s, agc_r,
     rsc_s, rsc_r, rsn_s, rsn_r, rsf_s, rsf_r,
     pg_s, pg_r, xs_s, xs_r, xc_s, xc_r,
@@ -54,8 +54,9 @@
     sibling = at(0, core=1 - c)
     far_z = (8, -8, 4, -4)
 
-    load_w = pltpu.make_async_copy(w_hbm, w, w_sem)
-    load_w.start()
+    load_x = pltpu.make_async_copy(x_hbm, xt.at[yh, g0, n, c], in_sem.at[0])
+    load_w = pltpu.make_async_copy(w_hbm, w, in_sem.at[1])
+    load_h = pltpu.make_async_copy(h_hbm, hg, in_sem.at[2])
 
     barrier = pltpu.get_barrier_semaphore()
     for dz in far_z:
@@ -67,9 +68,11 @@
     for r in range(1, NDP):
         pl.semaphore_signal(barrier, inc=1, device_id=((dp - r + NDP) % NDP, mp), device_id_type=MESH)
 
-    xt[yh, g0, n, c] = x_ref[...].astype(F32).T.astype(BF16)
-    hgt[...] = h_ref[...].astype(F32).T
+    load_x.start()
+    load_w.start()
+    load_h.start()
     acc[...] = jnp.zeros_like(acc)
+    load_x.wait()
     pl.semaphore_wait(barrier, 4 + 7 + 1 + 7)
 
     def ag_far(k):
@@ -103,8 +106,8 @@
         ref = xt.at[:, g, :, core]
         return send(ref, ref, agc_s.at[g], agc_r.at[g], sibling)
 
-    def rows_of(y, g):
-        return pl.ds(pl.multiple_of((y * NG + g) * BLK, BLK), BLK)
+    def weights_of(y, g):
+        return w[:, pl.ds(pl.multiple_of((y * NG + g) * BLK, BLK), BLK)]
 
     def pass_on(i):
         g = group(ring(i))
@@ -116,11 +119,14 @@
         ag_core(g, 1 - c).wait_recv()
         total = acc[...]
         for y in range(NY):
-            total += lax.dot_general(
-                w[rows_of(y, g), :], xt[y, g].reshape(BLK, TOK),
-                (((0,), (0,)), ((), ())), preferred_element_type=F32,
+            total += jnp.dot(
+                weights_of(y, g), xt[y, g].reshape(BLK, TOK), preferred_element_type=F32
             )
         acc[...] = total
+
+    def turn(b):
+        at_b = pl.ds(pl.multiple_of(b * BLK, BLK), BLK)
+        wt[at_b, :] = w[:, at_b].T
 
     def loop(low, high, *steps):
         def body(i, carry):
@@ -133,6 +139,9 @@
     for k in range(4):
         ag_far(k).start()
     ag_near_start(0)
+    load_w.wait()
+    load_h.wait()
+    loop(0, NY * NG, turn)
     ag_far_got(0)
     ag_far_got(1)
     for k in (6, 4, 5):
@@ -140,7 +149,6 @@
     ag_far_got(2)
     ag_far_got(3)
     loop(1, 5, ag_near_start)
-    load_w.wait()
     pass_on(0)
     ag_far_got(4)
     ag_far_got(5)
@@ -152,7 +160,7 @@
     multiply(6)
     multiply(7)
 
-    pga[dp] = (hgt[...] * gelu_slope(acc[...])).astype(BF16)
+    pga[dp] = (hg[...].astype(F32) * gelu_slope(acc[...])).astype(BF16)
     pgt = pga[dp]
 
     def rs_core(g):
@@ -161,7 +169,8 @@
     def partial(i):
         g = group(ring(i))
         for y in range(NY):
-            part = jnp.dot(w[rows_of(y, g), :], pgt, preferred_element_type=F32)
+            rows = pl.ds(pl.multiple_of((y * NG + g) * BLK, BLK), BLK)
+            part = jnp.dot(wt[rows, :], pgt, preferred_element_type=F32)
             tp[y, g] = part.astype(BF16).reshape(NN, NC, CH, TOK)
         rs_core(g).start()
 
@@ -230,6 +239,19 @@
     partial(0)
     loop(1, 3, pair_up)
     pair_up(0)
+    for k in range(7):
+        ag_far(k).wait_send()
+
+    def ag_sent(g):
+        for e in NEAR:
+            ag_near(g, e).wait_send()
+        ag_core(g, c).wait_send()
+
+    loop(0, NG, ag_sent)
+
+    rs_far_start(0, near_sum(3))
+    rs_far_start(1, near_sum(-3))
+    rs_far_start(2, near_sum(4))
     own_copies = []
     for half in range(2):
         y, g = slice_of(dp, half)
@@ -239,30 +261,16 @@
         pg_send(r).start()
     for r in range(1, NDP):
         xs_send(r).start()
-
-    for k in range(7):
-        ag_far(k).wait_send()
-
-    def ag_sent(g):
-        for e in NEAR:
-            ag_near(g, e).wait_send()
-        ag_core(g, c).wait_send()
-
-    loop(0, NG, ag_sent)
-
-    rs_far_start(0, near_sum(3))
-    rs_far_start(1, near_sum(-3))
-    rs_far_start(2, near_sum(4))
     rs_far_start(6, near_sum(-2 * sgn))
     ahead = near_sum(2 * sgn)
     right, left = near_sum(1), near_sum(-1)
     mine = near_sum(0)
+    rs_far_start(5, ahead + rs_far_got(2))
+    rs_far_start(3, right + rs_far_got(0))
+    rs_far_start(4, left + rs_far_got(1))
     for r in range(1, NDP):
         xs_got(r)
         xc_copy(r, c).start()
-    rs_far_start(3, right + rs_far_got(0))
-    rs_far_start(4, left + rs_far_got(1))
-    rs_far_start(5, ahead + rs_far_got(2))
 
     for copy in own_copies:
         copy.wait()
@@ -270,18 +278,17 @@
         pg_got(r)
         xc_copy(r, 1 - c).wait_recv()
 
-    def weight_rows(i):
-        half, quarter = i // 2, i % 2
-        total = jnp.zeros((BLK // 2, HID), F32)
+    def weight_rows(half):
+        total = jnp.zeros((HID, BLK), F32)
         for p in range(NDP):
             total += lax.dot_general(
-                xs[p, half, pl.ds(2 * quarter, 2)].reshape(BLK // 2, TOK), pga[p],
+                pga[p], xs[p, half].reshape(BLK, TOK),
                 (((1,), (1,)), ((), ())), preferred_element_type=F32,
             )
-        wg[pl.ds(pl.multiple_of(i * (BLK // 2), BLK // 2), BLK // 2), :] = total
-
-    loop(0, 4, weight_rows)
-    store_wg = pltpu.make_async_copy(wg, wg_hbm, wg_sem)
+        wg[:, pl.ds(pl.multiple_of(half * BLK, BLK), BLK)] = total
+
+    loop(0, 2, weight_rows)
+    store_wg = pltpu.make_async_copy(wg, wg_hbm, out_sem.at[0])
     store_wg.start()
 
     def rs_sent(g):
@@ -297,31 +304,32 @@
 
     for k in (3, 4, 5, 6):
         mine += rs_far_got(k)
-    tok_ref[...] = mine.T.astype(BF16)
+    tok[...] = mine.astype(BF16)
+    store_tok = pltpu.make_async_copy(tok, tok_hbm, out_sem.at[1])
+    store_tok.start()
     for k in range(7):
         rs_far(k).wait_send()
     store_wg.wait()
+    store_tok.wait()
 
 
 def local(tokens_in, in_weight, hidden_grad):
     vmem, dma = pltpu.VMEM, pltpu.SemaphoreType.DMA
     features = in_weight.shape[0]
-    return pl.pallas_call(
+    token_rows, weight_cols = pl.pallas_call(
         kernel,
         out_shape=(
-            jax.ShapeDtypeStruct((TOK, CH), BF16),
-            jax.ShapeDtypeStruct((features // NDP, HID), F32),
+            jax.ShapeDtypeStruct((CH, TOK), BF16),
+            jax.ShapeDtypeStruct((HID, features // NDP), F32),
         ),
-        in_specs=[
-            pl.BlockSpec(memory_space=pltpu.VMEM),
-            pl.BlockSpec(memory_space=pl.ANY),
-            pl.BlockSpec(memory_space=pltpu.VMEM),
-        ],
-        out_specs=(pl.BlockSpec(memory_space=pltpu.VMEM), pl.BlockSpec(memory_space=pl.ANY)),
+        in_specs=[pl.BlockSpec(memory_space=pl.ANY)] * 3,
+        out_specs=(pl.BlockSpec(memory_space=pl.ANY),) * 2,
         scratch_shapes=[
+            vmem((HID, features), BF16),
             vmem((features, HID), BF16),
+            vmem((HID, TOK), BF16),
+            vmem((CH, TOK), BF16),
             vmem((NY, NG, NN, NC, CH, TOK), BF16),
-            vmem((HID, TOK), F32),
             vmem((HID, TOK), F32),
             vmem((NY, NG, NN, NC, CH, TOK), BF16),
             vmem((NY, NG, NN, CH, TOK), BF16),
@@ -331,19 +339,20 @@
             vmem((7, CH, TOK), BF16),
             vmem((NDP, 2, NN, NC, CH, TOK), BF16),
             vmem((NDP, HID, TOK), BF16),
-            vmem((features // NDP, HID), F32),
-            dma, dma, dma((2,)),
+            vmem((HID, features // NDP), F32),
+            dma((3,)), dma((2,)), dma((2,)),
             dma((7,)), dma((7,)), dma((NG, 7)), dma((NG, 7)), dma((NG,)), dma((NG,)),
             dma((NG,)), dma((NG,)), dma((NG, 7)), dma((NG, 7)), dma((7,)), dma((7,)),
             dma((7,)), dma((7,)), dma((7,)), dma((7,)), dma((7,)), dma((7,)),
         ],
         compiler_params=pltpu.CompilerParams(
-            collective_id=0, has_side_effects=True, vmem_limit_bytes=40 * 2**20
+            collective_id=0, has_side_effects=True, vmem_limit_bytes=63 * 2**20
         ),
         cost_estimate=pl.CostEstimate(
             flops=6 * TOK * features * HID, bytes_accessed=4 * 2**20, transcendentals=2 * TOK * HID
         ),
-    )(tokens_in, in_weight, hidden_grad)
+    )(tokens_in.T, in_weight.T, hidden_grad.T)
+    return token_rows.T, weight_cols.T
 
 
 def solution(mesh):

time: 93.8 us -> 83.4 us (0.89); the launches traced: 92 us -> 83.2 us
  local copies, waits for them, and re-layouts: 8.5 us -> 3.22 us
  Pallas kernels: 82.9 us -> 79.3 us
    pallas_call x1, Pallas kernels: 82.9 us -> 79.3 us  [local(): pl.pallas_call(kernel, out_shape=(jax.ShapeDtypeStruct((CH, TOK), BF16),...]
    pallas_call x2 -> x0, local copies, waits for them, and re-layouts: 2.88 us -> none  [local(): pl.pallas_call(kernel, out_shape=(jax.ShapeDtypeStruct((TOK, CH), BF16),...]
    unnamed x5 -> x2, local copies, waits for them, and re-layouts: 5.61 us -> 3.22 us
where the time goes in v2:
time: 83.4 us; the launch traced here: 83.2 us
  Pallas kernels  79.3 us (95%)
  local copies, waits for them, and re-layouts  3.22 us (4%)
    pallas_call x1, Pallas kernels, local(): pl.pallas_call(kernel, out_shape=(jax.ShapeDtypeStruct((CH, TOK), BF16),...  79.3 us
    unnamed x2, local copies, waits for them, and re-layouts  3.22 us

profile of v2, /device:TPU:1, one launch (start us, length us, event | category | flops | bytes accessed | tf_op | source)
XLA Modules:
  0.0 83.2 jit_solution(9731024735732744404)
XLA Ops:
  0.6 79.3 %shard_map.50 = (bf16[48,128]{1,0:T(8,128)(2,1)}, f32[192,768]{1,0:T(8,128)}) custom-call(bf16[48,128]{1,0:T(8,128)(2,1)} %bitcast.9, bf16[192,6144]{1,0:T(8,128)(2,1)} %bitcast.7, bf16[192,128]{1,0:T(8,128)(2,1)} %bitcast.8), custom_call_target="tpu_custom_call" | custom-call | flops 905969664 | bytes 4194304 | tf_op jit(solution)/shard_map/pallas_call | solution.py:319
  79.9 1.3 %copy.7 = bf16[128,48]{0,1:T(8,128)(2,1)} copy(bf16[128,48]{0,1:T(8,128)(2,1)} %bitcast.6) | data formatting | bytes 24576
  81.2 1.9 %copy.8 = f32[768,192]{0,1:T(8,128)} copy(f32[768,192]{0,1:T(8,128)} %bitcast.5) | data formatting | bytes 1179648

commit v3 on v2

--- a/solution.py
+++ b/solution.py
@@ -51,6 +51,12 @@
     def group(offset):
         return (g0 + offset + NG) % NG
 
+    def target(r):
+        return ((dp // 4 + r // 4) % 2) * 4 + (dp % 4 + r % 4) % 4
+
+    def source(r):
+        return ((dp // 4 + r // 4) % 2) * 4 + (dp % 4 - r % 4 + 4) % 4
+
     sibling = at(0, core=1 - c)
     far_z = (8, -8, 4, -4)
 
@@ -66,7 +72,7 @@
         pl.semaphore_signal(barrier, inc=1, device_id=at(-dz, dy), device_id_type=MESH)
     pl.semaphore_signal(barrier, inc=1, device_id=sibling, device_id_type=MESH)
     for r in range(1, NDP):
-        pl.semaphore_signal(barrier, inc=1, device_id=((dp - r + NDP) % NDP, mp), device_id_type=MESH)
+        pl.semaphore_signal(barrier, inc=1, device_id=(source(r), mp), device_id_type=MESH)
 
     load_x.start()
     load_w.start()
@@ -212,25 +218,61 @@
         return p // 4, 2 * (p % 4) + half
 
     def pg_send(r):
-        return send(pga.at[dp], pga.at[dp], pg_s.at[r - 1], pg_r.at[r - 1], ((dp + r) % NDP, mp))
+        return send(pga.at[dp], pga.at[dp], pg_s.at[r - 1], pg_r.at[r - 1], (target(r), mp))
 
     def pg_got(r):
-        ref = pga.at[(dp - r + NDP) % NDP]
+        ref = pga.at[source(r)]
         send(ref, ref, pg_s.at[r - 1], pg_r.at[r - 1], sibling).wait_recv()
 
     def xs_send(r):
-        to = (dp + r) % NDP
+        to = target(r)
         y, g = slice_of(to, c)
         return send(xt.at[y, g], xs.at[dp, c], xs_s.at[r - 1], xs_r.at[r - 1], (to, mp))
 
     def xs_got(r):
-        ref = xs.at[(dp - r + NDP) % NDP, c]
+        ref = xs.at[source(r), c]
         send(ref, ref, xs_s.at[r - 1], xs_r.at[r - 1], sibling).wait_recv()
 
     def xc_copy(r, half):
-        ref = xs.at[(dp - r + NDP) % NDP, half]
+        ref = xs.at[source(r), half]
         return send(ref, ref, xc_s.at[r - 1], xc_r.at[r - 1], sibling)
 
+    def dp_send(low, high):
+        for r in range(low, high):
+            pg_send(r).start()
+        for r in range(low, high):
+            xs_send(r).start()
+
+    def pass_halves(low, high):
+        for r in range(low, high):
+            xs_got(r)
+            xc_copy(r, c).start()
+
+    def weight_part(parts, first):
+        def rows(half):
+            cols = pl.ds(pl.multiple_of(half * BLK, BLK), BLK)
+            total = jnp.zeros((HID, BLK), F32) if first else wg[:, cols]
+            for r in parts:
+                p = source(r)
+                total += lax.dot_general(
+                    pga[p], xs[p, half].reshape(BLK, TOK),
+                    (((1,), (1,)), ((), ())), preferred_element_type=F32,
+                )
+            wg[:, cols] = total
+
+        others = [r for r in parts if r]
+        for r in others:
+            pg_got(r)
+        rows(c)
+        for r in others:
+            xc_copy(r, 1 - c).wait_recv()
+        rows(1 - c)
+
+    own_copies = []
+    for half in range(2):
+        y, g = slice_of(dp, half)
+        own_copies.append(pltpu.make_async_copy(xt.at[y, g], xs.at[dp, half], own_sem.at[half]))
+        own_copies[-1].start()
     loop(5, 8, partial)
     loop(3, 5, partial)
     loop(5, 8, pair_up)
@@ -239,6 +281,7 @@
     partial(0)
     loop(1, 3, pair_up)
     pair_up(0)
+    dp_send(1, 4)
     for k in range(7):
         ag_far(k).wait_send()
 
@@ -252,51 +295,32 @@
     rs_far_start(0, near_sum(3))
     rs_far_start(1, near_sum(-3))
     rs_far_start(2, near_sum(4))
-    own_copies = []
-    for half in range(2):
-        y, g = slice_of(dp, half)
-        own_copies.append(pltpu.make_async_copy(xt.at[y, g], xs.at[dp, half], own_sem.at[half]))
-        own_copies[-1].start()
-    for r in range(1, NDP):
-        pg_send(r).start()
-    for r in range(1, NDP):
-        xs_send(r).start()
+    dp_send(4, 8)
+    pass_halves(1, 4)
     rs_far_start(6, near_sum(-2 * sgn))
     ahead = near_sum(2 * sgn)
     right, left = near_sum(1), near_sum(-1)
     mine = near_sum(0)
+    for copy in own_copies:
+        copy.wait()
+    weight_part((0, 1, 2, 3), True)
+
     rs_far_start(5, ahead + rs_far_got(2))
     rs_far_start(3, right + rs_far_got(0))
     rs_far_start(4, left + rs_far_got(1))
-    for r in range(1, NDP):
-        xs_got(r)
-        xc_copy(r, c).start()
-
-    for copy in own_copies:
-        copy.wait()
-    for r in range(1, NDP):
-        pg_got(r)
-        xc_copy(r, 1 - c).wait_recv()
-
-    def weight_rows(half):
-        total = jnp.zeros((HID, BLK), F32)
-        for p in range(NDP):
-            total += lax.dot_general(
-                pga[p], xs[p, half].reshape(BLK, TOK),
-                (((1,), (1,)), ((), ())), preferred_element_type=F32,
-            )
-        wg[:, pl.ds(pl.multiple_of(half * BLK, BLK), BLK)] = total
-
-    loop(0, 2, weight_rows)
+
+    def rs_sent(g):
+        for e in NEAR:
+            rs_near(g, e).wait_send()
+        rs_core(g).wait_send()
+
+    loop(0, NG, rs_sent)
+
+    pass_halves(4, 8)
+    weight_part((4, 5, 6, 7), False)
     store_wg = pltpu.make_async_copy(wg, wg_hbm, out_sem.at[0])
     store_wg.start()
 
-    def rs_sent(g):
-        for e in NEAR:
-            rs_near(g, e).wait_send()
-        rs_core(g).wait_send()
-
-    loop(0, NG, rs_sent)
     for r in range(1, NDP):
         pg_send(r).wait_send()
         xs_send(r).wait_send()
@@ -311,6 +335,17 @@
         rs_far(k).wait_send()
     store_wg.wait()
     store_tok.wait()
+
+
+def store(tok_in, wg_in, tok_hbm, wg_hbm, sem):
+    copies = [
+        pltpu.make_async_copy(wg_in, wg_hbm, sem.at[0]),
+        pltpu.make_async_copy(tok_in, tok_hbm, sem.at[1]),
+    ]
+    for copy in copies:
+        copy.start()
+    for copy in copies:
+        copy.wait()
 
 
 def local(tokens_in, in_weight, hidden_grad):
@@ -352,6 +387,16 @@
             flops=6 * TOK * features * HID, bytes_accessed=4 * 2**20, transcendentals=2 * TOK * HID
         ),
     )(tokens_in.T, in_weight.T, hidden_grad.T)
+    token_rows, weight_cols = pl.pallas_call(
+        store,
+        out_shape=(
+            jax.ShapeDtypeStruct(token_rows.shape, BF16),
+            jax.ShapeDtypeStruct(weight_cols.shape, F32),
+        ),
+        in_specs=[pl.BlockSpec(memory_space=pltpu.VMEM)] * 2,
+        out_specs=(pl.BlockSpec(memory_space=pl.ANY),) * 2,
+        scratch_shapes=[dma((2,))],
+    )(token_rows, weight_cols)
     return token_rows.T, weight_cols.T
 
 

time: 83.4 us -> 80.8 us (0.969)
  local copies, waits for them, and re-layouts: 3.22 us -> 0 us
    unnamed x2 -> x0, local copies, waits for them, and re-layouts: 3.22 us -> none
    pallas_call x0 -> x1, Pallas kernels: none -> 1.91 us  [local(): pl.pallas_call(store, out_shape=(jax.ShapeDtypeStruct(token_rows.shape, B...]
    pallas_call x1, Pallas kernels: 79.3 us -> 78 us  [local(): pl.pallas_call(kernel, out_shape=(jax.ShapeDtypeStruct((CH, TOK), BF16),...]
where the time goes in v3:
time: 80.8 us; the launch traced here: 80.5 us
  Pallas kernels  79.9 us (99%)
    pallas_call x1, Pallas kernels, local(): pl.pallas_call(kernel, out_shape=(jax.ShapeDtypeStruct((CH, TOK), BF16),...  78 us
    pallas_call x1, Pallas kernels, local(): pl.pallas_call(store, out_shape=(jax.ShapeDtypeStruct(token_rows.shape, B...  1.91 us

profile of v3, /device:TPU:1, one launch (start us, length us, event | category | flops | bytes accessed | tf_op | source)
XLA Modules:
  0.0 80.5 jit_solution(11487876709987954129)
XLA Ops:
  0.6 78.0 %shard_map.50 = (bf16[48,128]{1,0:T(8,128)(2,1)}, f32[192,768]{1,0:T(8,128)}) custom-call(bf16[48,128]{1,0:T(8,128)(2,1)} %bitcast.8, bf16[192,6144]{1,0:T(8,128)(2,1)} %bitcast.5, bf16[192,128]{1,0:T(8,128)(2,1)} %bitcast.7), custom_call_target="tpu_custom_call" | custom-call | flops 905969664 | bytes 4194304 | tf_op jit(solution)/shard_map/pallas_call | solution.py:354
  78.6 1.9 %shard_map.51 = (bf16[48,128]{1,0:T(8,128)(2,1)}, f32[192,768]{1,0:T(8,128)}) custom-call(bf16[48,128]{1,0:T(8,128)(2,1)} %get-tuple-element.6.tok_in, f32[192,768]{1,0:T(8,128)} %get-tuple-element.7.wg_in), custom_call_target="tpu_custom_call" | custom-call | tf_op jit(solution)/shard_map/pallas_call | solution.py:390

commit v4 on v3

--- a/solution.py
+++ b/solution.py
@@ -239,9 +239,9 @@
 
     def dp_send(low, high):
         for r in range(low, high):
+            xs_send(r).start()
+        for r in range(low, high):
             pg_send(r).start()
-        for r in range(low, high):
-            xs_send(r).start()
 
     def pass_halves(low, high):
         for r in range(low, high):

time: 80.8 us -> 79.5 us (0.984); the launches traced: 80.5 us -> 78.3 us
  Pallas kernels: 79.9 us -> 77.7 us
    pallas_call x1, Pallas kernels: 78 us -> 75.7 us  [local(): pl.pallas_call(kernel, out_shape=(jax.ShapeDtypeStruct((CH, TOK), BF16),...]
where the time goes in v4:
time: 79.5 us; the launch traced here: 78.3 us
  Pallas kernels  77.7 us (98%)
    pallas_call x1, Pallas kernels, local(): pl.pallas_call(kernel, out_shape=(jax.ShapeDtypeStruct((CH, TOK), BF16),...  75.7 us
    pallas_call x1, Pallas kernels, local(): pl.pallas_call(store, out_shape=(jax.ShapeDtypeStruct(token_rows.shape, B...  1.91 us

profile of v4, /device:TPU:1, one launch (start us, length us, event | category | flops | bytes accessed | tf_op | source)
XLA Modules:
  0.0 78.3 jit_solution(10542769990199504704)
XLA Ops:
  0.6 75.7 %shard_map.50 = (bf16[48,128]{1,0:T(8,128)(2,1)}, f32[192,768]{1,0:T(8,128)}) custom-call(bf16[48,128]{1,0:T(8,128)(2,1)} %bitcast.8, bf16[192,6144]{1,0:T(8,128)(2,1)} %bitcast.5, bf16[192,128]{1,0:T(8,128)(2,1)} %bitcast.7), custom_call_target="tpu_custom_call" | custom-call | flops 905969664 | bytes 4194304 | tf_op jit(solution)/shard_map/pallas_call | solution.py:354
  76.4 1.9 %shard_map.51 = (bf16[48,128]{1,0:T(8,128)(2,1)}, f32[192,768]{1,0:T(8,128)}) custom-call(bf16[48,128]{1,0:T(8,128)(2,1)} %get-tuple-element.6.tok_in, f32[192,768]{1,0:T(8,128)} %get-tuple-element.7.wg_in), custom_call_target="tpu_custom_call" | custom-call | tf_op jit(solution)/shard_map/pallas_call | solution.py:390
